TPU v7x, 32 devices: a whole 2x2x4 slice. The times are simulated.
32 devices in a mesh: occ: 4 (over y, core), virt: 4 (over z), rep: 2 (over x).
Axes of the slice: x: 2, y: 2, z: 4, core: 2. Of those that a mesh axis runs over, the one named last changes fastest.
Arguments:
- amplitudes: bfloat16 [4096, 1920], P(('occ', 'rep'), 'virt'), may hold values from -6 to 6
- integrals: bfloat16 [1920, 1024], P(('occ', 'rep'), 'virt'), may hold values from -0.375 to 0.375
- cd_irrep: int32 [1920], P(('occ', 'rep')), may hold values from 0 to 7
- ab_irrep: int32 [1024], P('virt'), may hold values from 0 to 7
Outputs:
- residual: float32 [4096, 1024], P(('occ', 'rep'), 'virt')
Inputs may be any that keep to these rules, and one draw needn't show every extreme that they name: `cd_irrep`: irreps of the eight D2h irreducible representations. `ab_irrep`: irreps of the eight D2h irreducible representations.
All inputs are finite; a program needn't handle non-finite values.
Results may differ from a plain program's by a relative error of at most 0.0003.
Values may be sent and summed in bfloat16 or wider, within the bound.
A program may use at most 64 MiB of HBM per device.

v0:
```python
import jax
import jax.numpy as jnp
from jax import lax
from jax.sharding import PartitionSpec as P


def local(amplitudes, integrals, cd_irrep, ab_irrep):
    allowed = cd_irrep[:, None] == ab_irrep[None, :]
    masked = jnp.where(allowed, integrals, jnp.zeros_like(integrals))
    rows = lax.all_gather(masked, ("occ", "rep"), axis=0, tiled=True)
    columns = lax.all_gather(amplitudes, "virt", axis=1, tiled=True)
    return jnp.dot(columns, rows, preferred_element_type=jnp.float32)


def solution(mesh):
    in_specs = (P(("occ", "rep"), "virt"), P(("occ", "rep"), "virt"), P(("occ", "rep")), P("virt"))
    out_specs = P(("occ", "rep"), "virt")
    return jax.shard_map(local, mesh=mesh, in_specs=in_specs, out_specs=out_specs, check_vma=False)
```

profile of v0, /device:TPU:0, one launch (start us, length us, event | category | flops | bytes accessed | tf_op | source)
XLA Modules:
  0.0 65.3 jit_solution(85361365989300138)
XLA Ops:
  6.5 0.0 all-gather.2.cloned.1.call-start
  6.5 0.7 %all-gather.2.cloned.1.call-update = ((bf16[512,480]{0,1:T(8,128)(2,1)}), bf16[512,1920]{0,1:T(8,128)(2,1)}) async-update(((), (), s32[]{:S(2)}) %all-gather.2.cloned.1.call-start, bf16[512,480]{0,1:T(8,128)(2,1)} %param.4) | async-update | bytes 2949144
  7.3 1.0 %compare_select_fusion = bf16[240,256]{1,0:T(8,128)(2,1)S(1)} fusion(bf16[240,256]{1,0:T(8,128)(2,1)} %param.5, s32[256]{0:T(256)} %param.7, s32[240]{0:T(256)} %param.6), kind=kLoop, calls=%fused_computation.1 | loop fusion | flops 122880 | bytes 247744 | tf_op jit(solution)/shard_map/jit(_where)/select_n | solution.py:9
  8.3 20.8 %all_gather.6 = bf16[1920,256]{1,0:T(8,128)(2,1)S(1)} all-gather(bf16[240,256]{1,0:T(8,128)(2,1)S(1)} %compare_select_fusion), channel_id=1, replica_groups=mesh['occ'=4,'virt'=4,'rep'=2] {'occ','rep'}, dimensions={0}, use_global_device_ids=true | all-gather | bytes 1105920 | tf_op jit(solution)/shard_map/all_gather | solution.py:10
  29.1 26.2 %all-gather.2.cloned.1.call-done = bf16[512,1920]{0,1:T(8,128)(2,1)} async-done(((bf16[512,480]{0,1:T(8,128)(2,1)}), bf16[512,1920]{0,1:T(8,128)(2,1)}) %all-gather.2.cloned.1.call-update) | async-done | bytes 1966096 | tf_op jit(solution)/shard_map/all_gather | solution.py:11
  55.2 2.3 %convolution_bitcast_fusion = f32[512,256]{0,1:T(8,128)S(1)} fusion(bf16[1920,256]{1,0:T(8,128)(2,1)S(1)} %all_gather.6, bf16[512,1920]{0,1:T(8,128)(2,1)} %all-gather.2.cloned.1.call-done), kind=kOutput, calls=%fused_computation | convolution fusion | flops 503316480 | bytes 3473408 | tf_op jit(solution)/shard_map/dot_general | solution.py:12
  57.5 1.0 %copy.5 = f32[512,256]{1,0:T(8,128)} copy(f32[512,256]{0,1:T(8,128)S(1)} %convolution_bitcast_fusion) | data formatting | bytes 1048576 | tf_op jit(solution)/shard_map/dot_general | solution.py:12
Async XLA Ops:
  6.5 48.7 %all-gather.2.cloned.1.call-start = ((), (), s32[]{:S(2)}) async-start(), calls=%async_computation | async-start | bytes 2457600 | tf_op jit(solution)/shard_map/all_gather | solution.py:11
Sparse Core Ops, SparseCore 0:
  8.9 46.2 all-gather.1
where the time goes:
time: 65.5 us; the launch traced here: 65.3 us
  waiting for transfers between devices  26.9 us (41%)
  blocking collectives  20.8 us (32%)
  between operations  13.4 us (20%)
  matrix products  2.26 us (3%)
  other arithmetic  1.02 us (2%)
  local copies, waits for them, and re-layouts  1 us (2%)
    all_gather x1, waiting for transfers between devices, local(): columns = lax.all_gather(amplitudes, 'virt', axis=1, tiled=True)  26.2 us
    all_gather x1, blocking collectives, local(): rows = lax.all_gather(masked, ('occ', 'rep'), axis=0, tiled=True)  20.8 us
    dot_general x1, matrix products, local(): return jnp.dot(columns, rows, preferred_element_type=jnp.float32)  2.26 us
  transfers between devices with their start and end apart: 1, of which 1 were waited for; matrix products, arithmetic and copies ran while one was open for 2% of the time, Pallas kernels for 0%

commit v1 on v0

v1 whole, which is shorter than its diff:
```python
import functools

import jax
import jax.numpy as jnp
from jax import lax
from jax.experimental import pallas as pl
from jax.experimental.pallas import tpu as pltpu
from jax.sharding import PartitionSpec as P

MESH = pl.DeviceIdType.MESH
NV = 4
NO = 4
NR = 2
CHUNKS = 4
ORDER = ((3, 2, 1, 0), (3, 0, 2, 1), (0, 3, 1, 2), (0, 1, 2, 3))
PEERS = [(do, dr) for do in range(NO) for dr in range(NR) if (do, dr) != (0, 0)]


def schedule(zz):
    steps = []
    if zz in (0, NV - 1):
        for v in ORDER[zz][:-1]:
            steps += [(v, c) for c in range(CHUNKS)]
    else:
        a, b, near, _ = ORDER[zz]
        timed = []
        for c in range(CHUNKS):
            timed += [(c, 0, a, c), (c + 1.5, 1, b, c), (c + CHUNKS + 0.7, 2, near, c)]
        steps = [(v, c) for _, _, v, c in sorted(timed)]
    return steps + [(zz, c) for c in range(CHUNKS)]


def kernel(t_ref, i_ref, cd_ref, ab_ref, out_ref, masked, ints, full, psend, ssend, precv, srecv,
           mine_send, mine_recv, relay_send, relay_recv, p_ssem, s_ssem, p_rsem, s_rsem):
    o, z, r = lax.axis_index("occ"), lax.axis_index("virt"), lax.axis_index("rep")
    core = o % 2
    half = o // 2
    rows, depth = t_ref.shape
    chunk = rows // CHUNKS
    part = depth // NR

    barrier = pltpu.get_barrier_semaphore()
    friends = 0
    for do, dr in PEERS:
        pl.semaphore_signal(barrier, inc=1, device_id=((o + do) % NO, z, (r + dr) % NR), device_id_type=MESH)
        friends += 1
    for dz in range(1, NV):
        for do in (0, 2):
            pl.semaphore_signal(barrier, inc=1, device_id=((o + do) % NO, (z + dz) % NV, r), device_id_type=MESH)
            friends += 1

    cd = cd_ref[...]
    ab = ab_ref[...]
    one_cd = (lax.broadcasted_iota(jnp.int32, (8, cd.shape[1]), 0) == cd).astype(jnp.float32)
    one_ab = (lax.broadcasted_iota(jnp.int32, (8, ab.shape[1]), 0) == ab).astype(jnp.float32)
    same = lax.dot_general(one_cd, one_ab, (((0,), (0,)), ((), ())), preferred_element_type=jnp.float32)
    kept = jnp.where(same > 0.5, i_ref[...].astype(jnp.float32), 0.0).astype(jnp.bfloat16)
    width = kept.shape[1] // 2
    masked[0] = kept[:, :width]
    masked[1] = kept[:, width:]

    pl.semaphore_wait(barrier, friends)

    def first(h):
        return pltpu.make_async_remote_copy(
            src_ref=masked.at[h], dst_ref=ints.at[z, r, h], send_sem=mine_send.at[h], recv_sem=mine_recv.at[z],
            device_id=(2 * h + core, o, r), device_id_type=MESH)

    stays = [(z == o) & (half == h) for h in range(2)]
    for h in range(2):
        @pl.when(jnp.logical_not(stays[h]))
        def _():
            first(h).start()

        @pl.when(stays[h])
        def _():
            ints[z, r, h] = masked[h]

    relays = core == z % 2

    def hand(v, k):
        do, dr = PEERS[k]
        return pltpu.make_async_remote_copy(
            src_ref=ints.at[v, r, half], dst_ref=ints.at[v, r, half], send_sem=relay_send.at[v, k],
            recv_sem=relay_recv.at[v, r, half], device_id=((o + do) % NO, z, (r + dr) % NR), device_id_type=MESH)

    def relay(zz):
        @pl.when(relays)
        def _():
            for v in ORDER[zz]:
                arrival = pltpu.make_async_remote_copy(
                    src_ref=masked.at[0], dst_ref=ints.at[v, r, half], send_sem=mine_send.at[0],
                    recv_sem=mine_recv.at[v], device_id=((o + 1) % NO, z, r), device_id_type=MESH)
                if v == zz:
                    @pl.when(o != z)
                    def _():
                        arrival.wait_recv()
                else:
                    arrival.wait_recv()
                for k in range(len(PEERS)):
                    hand(v, k).start()

    def gathered(v):
        for rr in range(NR):
            for h in range(2):
                @pl.when(jnp.logical_not(relays & (r == rr) & (half == h)))
                def _():
                    pltpu.make_async_remote_copy(
                        src_ref=ints.at[v, rr, h], dst_ref=ints.at[v, rr, h], send_sem=relay_send.at[v, 0],
                        recv_sem=relay_recv.at[v, rr, h], device_id=((o + 1) % NO, z, r),
                        device_id_type=MESH).wait_recv()
                full[v, rr * part:(rr + 1) * part, h * width:(h + 1) * width] = ints[v, rr, h]

    def pass_on(zz, v, c):
        to = zz + 1 if v > zz else zz - 1
        slot = NV if (v < zz and v == to) else v
        where = dict(device_id=(o, to, r), device_id_type=MESH)
        return (
            pltpu.make_async_remote_copy(
                src_ref=psend.at[v, c], dst_ref=precv.at[slot, c], send_sem=p_ssem.at[v, c],
                recv_sem=p_rsem.at[slot, c], **where),
            pltpu.make_async_remote_copy(
                src_ref=ssend.at[v, c], dst_ref=srecv.at[slot, c], send_sem=s_ssem.at[v, c],
                recv_sem=s_rsem.at[slot, c], **where),
        )

    def arrived(slot, c):
        where = dict(device_id=(o, (z + 1) % NV, r), device_id_type=MESH)
        pltpu.make_async_remote_copy(
            src_ref=precv.at[slot, c], dst_ref=precv.at[slot, c], send_sem=p_ssem.at[0, c],
            recv_sem=p_rsem.at[slot, c], **where).wait_recv()
        pltpu.make_async_remote_copy(
            src_ref=srecv.at[slot, c], dst_ref=srecv.at[slot, c], send_sem=s_ssem.at[0, c],
            recv_sem=s_rsem.at[slot, c], **where).wait_recv()
        return precv[slot, c].astype(jnp.int32).astype(jnp.float32) * srecv[slot, c, 0:1, :]

    def line(zz):
        relay(zz)
        seen = set()
        for v, c in schedule(zz):
            if v not in seen:
                gathered(v)
                seen.add(v)
            at = slice(c * chunk, (c + 1) * chunk)
            total = jnp.dot(t_ref[at, :], full[v], preferred_element_type=jnp.float32)
            if v >= zz and zz > 0:
                total += arrived(v, c)
            if v < zz and zz < NV - 1:
                total += arrived(v, c)
            if v == zz and zz < NV - 1:
                total += arrived(NV, c)
            if v == zz:
                out_ref[at, :] = total
            else:
                most = jnp.maximum(jnp.max(jnp.abs(total), axis=0, keepdims=True), 1e-30)
                ssend[v, c] = jnp.broadcast_to(most * (1.0 / 32767.0), (8, total.shape[1]))
                psend[v, c] = jnp.round(total * (32767.0 / most)).astype(jnp.int32).astype(jnp.int16)
                for copy in pass_on(zz, v, c):
                    copy.start()
        for v, c in schedule(zz):
            if v != zz:
                for copy in pass_on(zz, v, c):
                    copy.wait_send()

        @pl.when(relays)
        def _():
            for v in ORDER[zz]:
                for k in range(len(PEERS)):
                    hand(v, k).wait_send()

    for zz in range(NV):
        @pl.when(z == zz)
        def _():
            line(zz)

    for h in range(2):
        @pl.when(jnp.logical_not(stays[h]))
        def _():
            first(h).wait_send()


def on_lines(amplitudes, integrals, cd_irrep, ab_irrep):
    rows, depth = amplitudes.shape
    part, width = integrals.shape
    chunk = rows // CHUNKS
    slots = NV + 1
    dma = pltpu.SemaphoreType.DMA
    return pl.pallas_call(
        kernel,
        out_shape=jax.ShapeDtypeStruct((rows, width), jnp.float32),
        in_specs=[pl.BlockSpec(memory_space=pltpu.VMEM)] * 4,
        out_specs=pl.BlockSpec(memory_space=pltpu.VMEM),
        scratch_shapes=[
            pltpu.VMEM((2, part, width // 2), jnp.bfloat16),
            pltpu.VMEM((NV, NR, 2, part, width // 2), jnp.bfloat16),
            pltpu.VMEM((NV, depth, width), jnp.bfloat16),
            pltpu.VMEM((NV, CHUNKS, chunk, width), jnp.int16),
            pltpu.VMEM((NV, CHUNKS, 8, width), jnp.float32),
            pltpu.VMEM((slots, CHUNKS, chunk, width), jnp.int16),
            pltpu.VMEM((slots, CHUNKS, 8, width), jnp.float32),
            dma((2,)), dma((NV,)), dma((NV, len(PEERS))), dma((NV, NR, 2)),
            dma((NV, CHUNKS)), dma((NV, CHUNKS)), dma((slots, CHUNKS)), dma((slots, CHUNKS)),
        ],
        compiler_params=pltpu.CompilerParams(
            collective_id=0, has_side_effects=True, vmem_limit_bytes=32 * 1024 * 1024),
        cost_estimate=pl.CostEstimate(
            flops=2 * rows * depth * NV * width, bytes_accessed=3 * rows * depth, transcendentals=0),
    )(amplitudes, integrals, cd_irrep.reshape(1, -1), ab_irrep.reshape(1, -1))


def by_gathers(amplitudes, integrals, cd_irrep, ab_irrep):
    allowed = cd_irrep[:, None] == ab_irrep[None, :]
    masked = jnp.where(allowed, integrals, jnp.zeros_like(integrals))
    rows = lax.all_gather(masked, ("occ", "rep"), axis=0, tiled=True)
    columns = lax.all_gather(amplitudes, "virt", axis=1, tiled=True)
    return jnp.dot(columns, rows, preferred_element_type=jnp.float32)


def solution(mesh):
    in_specs = (P(("occ", "rep"), "virt"), P(("occ", "rep"), "virt"), P(("occ", "rep")), P("virt"))
    out_specs = P(("occ", "rep"), "virt")
    lines = (mesh.shape["occ"], mesh.shape["virt"], mesh.shape["rep"]) == (NO, NV, NR)
    return jax.shard_map(on_lines if lines else by_gathers, mesh=mesh, in_specs=in_specs,
                         out_specs=out_specs, check_vma=False)
```

time: 65.5 us -> 39.9 us (0.61)
  Pallas kernels: 0 us -> 37.6 us
  waiting for transfers between devices: 26.9 us -> 0 us
  blocking collectives: 20.8 us -> 0 us
  between operations: 13.4 us -> 0.04 us
  matrix products: 2.26 us -> 0 us
  local copies, waits for them, and re-layouts: 1 us -> 2.08 us
  other arithmetic: 1.02 us -> 0 us
    pallas_call x0 -> x1, Pallas kernels: none -> 37.6 us  [on_lines(): pl.pallas_call(kernel, out_shape=jax.ShapeDtypeStruct((rows, width), jnp....]
    all_gather x1 -> x0, waiting for transfers between devices: 26.2 us -> none  [local(): columns = lax.all_gather(amplitudes, 'virt', axis=1, tiled=True)]
    all_gather x1 -> x0, blocking collectives: 20.8 us -> none  [local(): rows = lax.all_gather(masked, ('occ', 'rep'), axis=0, tiled=True)]
    dot_general x1 -> x0, matrix products: 2.26 us -> none  [local(): return jnp.dot(columns, rows, preferred_element_type=jnp.float32)]
    unnamed x0 -> x8, local copies, waits for them, and re-layouts: none -> 2.08 us
    select_n x1 -> x0, other arithmetic: 1.02 us -> none  [local(): masked = jnp.where(allowed, integrals, jnp.zeros_like(integrals))]
    dot_general x1 -> x0, local copies, waits for them, and re-layouts: 1 us -> none  [local(): return jnp.dot(columns, rows, preferred_element_type=jnp.float32)]
    unnamed x1 -> x0, waiting for transfers between devices: 0.71 us -> none
  transfers between devices with their start and end apart: 1 -> 0, of which waited for: 1 -> 0; matrix products, arithmetic and copies ran while one was open for 2% -> 0% of each run, Pallas kernels for 0% -> 0%
where the time goes in v1:
time: 39.9 us; the launch traced here: 39.7 us
  Pallas kernels  37.6 us (94%)
  local copies, waits for them, and re-layouts  2.08 us (5%)
    pallas_call x1, Pallas kernels, on_lines(): pl.pallas_call(kernel, out_shape=jax.ShapeDtypeStruct((rows, width), jnp....  37.6 us
    unnamed x8, local copies, waits for them, and re-layouts  2.08 us

profile of v1, /device:TPU:0, one launch (start us, length us, event | category | flops | bytes accessed | tf_op | source)
XLA Modules:
  0.0 39.7 jit_solution(5617696126207041163)
XLA Ops:
  0.0 0.0 copy-start
  0.0 0.0 copy-start.1
  0.0 0.0 copy-start.2
  0.0 1.3 %copy.5.t_ref = bf16[512,480]{1,0:T(8,128)(2,1)S(1)} copy(bf16[512,480]{0,1:T(8,128)(2,1)} %param.4) | data formatting | bytes 983040 | tf_op args[0]
  1.3 0.0 copy-done
  1.3 0.0 copy-done.1
  1.3 0.0 copy-done.2
  1.3 37.6 %shard_map.46 = f32[512,256]{1,0:T(8,128)S(1)} custom-call(bf16[512,480]{1,0:T(8,128)(2,1)S(1)} %copy.5.t_ref, bf16[240,256]{1,0:T(8,128)(2,1)S(1)} %copy-done, s32[1,240]{1,0:T(1,128)S(1)} %bitcast.2, s32[1,256]{1,0:T(1,128)S(1)} %bitcast.3), custom_call_target="tpu_custom_call" | custom-call | flops 503316480 | bytes 737280 | tf_op jit(solution)/shard_map/pallas_call | solution.py:188
  38.9 0.8 %copy.7 = f32[512,256]{1,0:T(8,128)} copy(f32[512,256]{1,0:T(8,128)S(1)} %shard_map.46) | data formatting | bytes 1048576
Async XLA Ops:
  0.0 1.3 %copy-start = (bf16[240,256]{1,0:T(8,128)(2,1)S(1)}, bf16[240,256]{1,0:T(8,128)(2,1)}, u32[]{:S(2)}) copy-start(bf16[240,256]{1,0:T(8,128)(2,1)} %i_ref.1) | copy-start | bytes 368644
  0.0 1.3 %copy-start.1 = (s32[240]{0:T(256)S(1)}, s32[240]{0:T(256)}, u32[]{:S(2)}) copy-start(s32[240]{0:T(256)} %param.6) | copy-start | bytes 2884
  0.0 1.3 %copy-start.2 = (s32[256]{0:T(256)S(1)}, s32[256]{0:T(256)}, u32[]{:S(2)}) copy-start(s32[256]{0:T(256)} %param.7) | copy-start | bytes 3076

commit v2 on v1

v2 whole, which is shorter than its diff:
```python
import functools

import jax
import jax.numpy as jnp
from jax import lax
from jax.experimental import pallas as pl
from jax.experimental.pallas import tpu as pltpu
from jax.sharding import PartitionSpec as P

MESH = pl.DeviceIdType.MESH
NV = 4
NO = 4
NR = 2
CHUNKS = 4
ORDER = ((3, 2, 1, 0), (3, 0, 2, 1), (0, 3, 1, 2), (0, 1, 2, 3))
PEERS = [(2, 0), (0, 1), (2, 1)]


def parts_of(zz, v):
    chunks = list(range(CHUNKS))
    late = v == zz or 0 < v < NV - 1
    return chunks[CHUNKS // 2:] + chunks[:CHUNKS // 2] if late else chunks


def schedule(zz):
    steps = []
    if zz in (0, NV - 1):
        for v in ORDER[zz][:-1]:
            steps += [(v, c) for c in parts_of(zz, v)]
    else:
        a, b, near, _ = ORDER[zz]
        timed = []
        for k in range(CHUNKS):
            timed += [(k, 0, a, parts_of(zz, a)[k]), (k + 1.5, 1, b, parts_of(zz, b)[k]),
                      (k + CHUNKS + 0.7, 2, near, parts_of(zz, near)[k])]
        steps = [(v, c) for _, _, v, c in sorted(timed)]
    return steps + [(zz, c) for c in parts_of(zz, zz)]


def kernel(t_ref, i_ref, cd_ref, ab_ref, out_ref, masked, both, ints, full, psend, ssend, precv, srecv, fin,
           mine_send, mine_recv, relay_send, relay_recv, p_ssem, s_ssem, p_rsem, s_rsem, t_sem, f_ssem, f_rsem):
    o, z, r = lax.axis_index("occ"), lax.axis_index("virt"), lax.axis_index("rep")
    core = o % 2
    half = o // 2
    other = 2 * half + 1 - core
    rows, depth = t_ref.shape
    chunk = 2 * rows // CHUNKS
    part = depth // NR

    barrier = pltpu.get_barrier_semaphore()
    friends = 0
    for dz in range(NV):
        for do in range(NO):
            if (dz, do) != (0, 0):
                pl.semaphore_signal(
                    barrier, inc=1, device_id=((o + do) % NO, (z + dz) % NV, r), device_id_type=MESH)
                friends += 1
    for do in (0, 2):
        pl.semaphore_signal(barrier, inc=1, device_id=((o + do) % NO, z, (r + 1) % NR), device_id_type=MESH)
        friends += 1

    cd = cd_ref[...]
    ab = ab_ref[...]
    one_cd = (lax.broadcasted_iota(jnp.int32, (8, cd.shape[1]), 0) == cd).astype(jnp.float32)
    one_ab = (lax.broadcasted_iota(jnp.int32, (8, ab.shape[1]), 0) == ab).astype(jnp.float32)
    same = lax.dot_general(one_cd, one_ab, (((0,), (0,)), ((), ())), preferred_element_type=jnp.float32)
    kept = jnp.where(same > 0.5, i_ref[...].astype(jnp.float32), 0.0).astype(jnp.bfloat16)
    width = kept.shape[1] // 2
    masked[0] = kept[:, :width]
    masked[1] = kept[:, width:]
    both[core] = t_ref[...]

    pl.semaphore_wait(barrier, friends)

    def first(h):
        return pltpu.make_async_remote_copy(
            src_ref=masked.at[h], dst_ref=ints.at[z, r], send_sem=mine_send.at[h], recv_sem=mine_recv.at[z],
            device_id=(3 * h, o, r), device_id_type=MESH)

    stays = [(z == o) & (o == 3 * h) for h in range(2)]
    for h in range(2):
        @pl.when(jnp.logical_not(stays[h]))
        def _():
            first(h).start()

        @pl.when(stays[h])
        def _():
            ints[z, r] = masked[h]

    def share(k):
        return pltpu.make_async_remote_copy(
            src_ref=both.at[k], dst_ref=both.at[k], send_sem=t_sem.at[0], recv_sem=t_sem.at[1],
            device_id=(other, z, r), device_id_type=MESH)

    share(core).start()

    relays = core == half

    def hand(v, k):
        do, dr = PEERS[k]
        return pltpu.make_async_remote_copy(
            src_ref=ints.at[v, r], dst_ref=ints.at[v, r], send_sem=relay_send.at[v, k],
            recv_sem=relay_recv.at[v, r], device_id=((o + do) % NO, z, (r + dr) % NR), device_id_type=MESH)

    def relay(zz, v):
        @pl.when(relays)
        def _():
            arrival = pltpu.make_async_remote_copy(
                src_ref=masked.at[0], dst_ref=ints.at[v, r], send_sem=mine_send.at[0],
                recv_sem=mine_recv.at[v], device_id=(other, z, r), device_id_type=MESH)
            if v == zz:
                @pl.when(o != z)
                def _():
                    arrival.wait_recv()
            else:
                arrival.wait_recv()
            for k in range(len(PEERS)):
                hand(v, k).start()

    def gathered(v):
        for rr in range(NR):
            @pl.when(jnp.logical_not(relays & (r == rr)))
            def _():
                pltpu.make_async_remote_copy(
                    src_ref=ints.at[v, rr], dst_ref=ints.at[v, rr], send_sem=relay_send.at[v, 0],
                    recv_sem=relay_recv.at[v, rr], device_id=(other, z, r), device_id_type=MESH).wait_recv()
            full[v, rr * part:(rr + 1) * part, :] = ints[v, rr]

    def pass_on(zz, v, c):
        to = zz + 1 if v > zz else zz - 1
        slot = NV if (v < zz and v == to) else v
        where = dict(device_id=(o, to, r), device_id_type=MESH)
        return (
            pltpu.make_async_remote_copy(
                src_ref=psend.at[v, c], dst_ref=precv.at[slot, c], send_sem=p_ssem.at[v, c],
                recv_sem=p_rsem.at[slot, c], **where),
            pltpu.make_async_remote_copy(
                src_ref=ssend.at[v, c], dst_ref=srecv.at[slot, c], send_sem=s_ssem.at[v, c],
                recv_sem=s_rsem.at[slot, c], **where),
        )

    def arrived(slot, c):
        where = dict(device_id=(other, z, r), device_id_type=MESH)
        pltpu.make_async_remote_copy(
            src_ref=precv.at[slot, c], dst_ref=precv.at[slot, c], send_sem=p_ssem.at[0, c],
            recv_sem=p_rsem.at[slot, c], **where).wait_recv()
        pltpu.make_async_remote_copy(
            src_ref=srecv.at[slot, c], dst_ref=srecv.at[slot, c], send_sem=s_ssem.at[0, c],
            recv_sem=s_rsem.at[slot, c], **where).wait_recv()
        return precv[slot, c].astype(jnp.int32).astype(jnp.float32) * srecv[slot, c, 0:1, :]

    def finish(hh, j):
        return pltpu.make_async_remote_copy(
            src_ref=fin.at[j], dst_ref=out_ref.at[j * chunk:(j + 1) * chunk, hh * width:(hh + 1) * width],
            send_sem=f_ssem.at[j], recv_sem=f_rsem.at[j], device_id=(other, z, r), device_id_type=MESH)

    per = CHUNKS // 2

    def line(zz):
        order = list(ORDER[zz])
        ahead = 2 if zz in (0, NV - 1) else NV
        for v in order[:ahead]:
            relay(zz, v)
        waiting = order[ahead:]
        seen, shared = set(), False
        for v, c in schedule(zz):
            if v not in seen:
                gathered(v)
                seen.add(v)
            cc, j = (core + c // per) % 2, c % per
            if c >= per and not shared:
                share(1 - core).wait_recv()
                shared = True
            total = jnp.dot(both[cc, j * chunk:(j + 1) * chunk, :], full[v], preferred_element_type=jnp.float32)
            if v >= zz and zz > 0:
                total += arrived(v, c)
            if v < zz and zz < NV - 1:
                total += arrived(v, c)
            if v == zz and zz < NV - 1:
                total += arrived(NV, c)
            if v == zz:
                for hh in range(2):
                    @pl.when(core == hh)
                    def _():
                        if c < per:
                            out_ref[j * chunk:(j + 1) * chunk, hh * width:(hh + 1) * width] = total
                        else:
                            fin[j] = total
                            finish(hh, j).start()
            else:
                most = jnp.maximum(jnp.max(jnp.abs(total), axis=0, keepdims=True), 1e-30)
                ssend[v, c] = jnp.broadcast_to(most * (1.0 / 32767.0), (8, total.shape[1]))
                psend[v, c] = jnp.round(total * (32767.0 / most)).astype(jnp.int32).astype(jnp.int16)
                for copy in pass_on(zz, v, c):
                    copy.start()
            if waiting and c == parts_of(zz, v)[-1]:
                relay(zz, waiting.pop(0))
        for v, c in schedule(zz):
            if v != zz:
                for copy in pass_on(zz, v, c):
                    copy.wait_send()

        @pl.when(relays)
        def _():
            for v in ORDER[zz]:
                for k in range(len(PEERS)):
                    hand(v, k).wait_send()

    for zz in range(NV):
        @pl.when(z == zz)
        def _():
            line(zz)

    for h in range(2):
        @pl.when(jnp.logical_not(stays[h]))
        def _():
            first(h).wait_send()
    share(core).wait_send()
    for hh in range(2):
        @pl.when(core == hh)
        def _():
            for j in range(per):
                finish(hh, j).wait_send()
                finish(1 - hh, j).wait_recv()


def on_lines(amplitudes, integrals, cd_irrep, ab_irrep):
    rows, depth = amplitudes.shape
    part, width = integrals.shape
    chunk, half = 2 * rows // CHUNKS, width // 2
    slots = NV + 1
    dma = pltpu.SemaphoreType.DMA
    return pl.pallas_call(
        kernel,
        out_shape=jax.ShapeDtypeStruct((rows, width), jnp.float32),
        in_specs=[pl.BlockSpec(memory_space=pltpu.VMEM)] * 4,
        out_specs=pl.BlockSpec(memory_space=pltpu.VMEM),
        scratch_shapes=[
            pltpu.VMEM((2, part, half), jnp.bfloat16),
            pltpu.VMEM((2, rows, depth), jnp.bfloat16),
            pltpu.VMEM((NV, NR, part, half), jnp.bfloat16),
            pltpu.VMEM((NV, depth, half), jnp.bfloat16),
            pltpu.VMEM((NV, CHUNKS, chunk, half), jnp.int16),
            pltpu.VMEM((NV, CHUNKS, 8, half), jnp.float32),
            pltpu.VMEM((slots, CHUNKS, chunk, half), jnp.int16),
            pltpu.VMEM((slots, CHUNKS, 8, half), jnp.float32),
            pltpu.VMEM((CHUNKS // 2, chunk, half), jnp.float32),
            dma((2,)), dma((NV,)), dma((NV, len(PEERS))), dma((NV, NR)),
            dma((NV, CHUNKS)), dma((NV, CHUNKS)), dma((slots, CHUNKS)), dma((slots, CHUNKS)),
            dma((2,)), dma((CHUNKS // 2,)), dma((CHUNKS // 2,)),
        ],
        compiler_params=pltpu.CompilerParams(
            collective_id=0, has_side_effects=True, vmem_limit_bytes=32 * 1024 * 1024),
        cost_estimate=pl.CostEstimate(
            flops=2 * rows * depth * NV * width, bytes_accessed=3 * rows * depth, transcendentals=0),
    )(amplitudes, integrals, cd_irrep.reshape(1, -1), ab_irrep.reshape(1, -1))


def by_gathers(amplitudes, integrals, cd_irrep, ab_irrep):
    allowed = cd_irrep[:, None] == ab_irrep[None, :]
    masked = jnp.where(allowed, integrals, jnp.zeros_like(integrals))
    rows = lax.all_gather(masked, ("occ", "rep"), axis=0, tiled=True)
    columns = lax.all_gather(amplitudes, "virt", axis=1, tiled=True)
    return jnp.dot(columns, rows, preferred_element_type=jnp.float32)


def solution(mesh):
    in_specs = (P(("occ", "rep"), "virt"), P(("occ", "rep"), "virt"), P(("occ", "rep")), P("virt"))
    out_specs = P(("occ", "rep"), "virt")
    lines = (mesh.shape["occ"], mesh.shape["virt"], mesh.shape["rep"]) == (NO, NV, NR)
    return jax.shard_map(on_lines if lines else by_gathers, mesh=mesh, in_specs=in_specs,
                         out_specs=out_specs, check_vma=False)
```

time: 39.9 us -> 37 us (0.927)
  the two profiles are of different devices: /device:TPU:0 before, /device:TPU:8 now
where the time goes in v2:
time: 37 us; the launch traced here: 36.8 us
  Pallas kernels  34.7 us (94%)
  local copies, waits for them, and re-layouts  2.08 us (6%)
    pallas_call x1, Pallas kernels, on_lines(): pl.pallas_call(kernel, out_shape=jax.ShapeDtypeStruct((rows, width), jnp....  34.7 us
    unnamed x8, local copies, waits for them, and re-layouts  2.08 us

profile of v2, /device:TPU:8, one launch (start us, length us, event | category | flops | bytes accessed | tf_op | source)
XLA Modules:
  0.0 36.8 jit_solution(13902258723494517248)
XLA Ops:
  0.0 0.0 copy-start
  0.0 0.0 copy-start.1
  0.0 0.0 copy-start.2
  0.0 1.3 %copy.5.t_ref = bf16[512,480]{1,0:T(8,128)(2,1)S(1)} copy(bf16[512,480]{0,1:T(8,128)(2,1)} %param.4) | data formatting | bytes 983040 | tf_op args[0]
  1.3 0.0 copy-done
  1.3 0.0 copy-done.1
  1.3 0.0 copy-done.2
  1.3 34.7 %shard_map.46 = f32[512,256]{1,0:T(8,128)S(1)} custom-call(bf16[512,480]{1,0:T(8,128)(2,1)S(1)} %copy.5.t_ref, bf16[240,256]{1,0:T(8,128)(2,1)S(1)} %copy-done, s32[1,240]{1,0:T(1,128)S(1)} %bitcast.2, s32[1,256]{1,0:T(1,128)S(1)} %bitcast.3), custom_call_target="tpu_custom_call" | custom-call | flops 503316480 | bytes 737280 | tf_op jit(solution)/shard_map/pallas_call | solution.py:233
  36.0 0.8 %copy.7 = f32[512,256]{1,0:T(8,128)} copy(f32[512,256]{1,0:T(8,128)S(1)} %shard_map.46) | data formatting | bytes 1048576
Async XLA Ops:
  0.0 1.3 %copy-start = (bf16[240,256]{1,0:T(8,128)(2,1)S(1)}, bf16[240,256]{1,0:T(8,128)(2,1)}, u32[]{:S(2)}) copy-start(bf16[240,256]{1,0:T(8,128)(2,1)} %i_ref.1) | copy-start | bytes 368644
  0.0 1.3 %copy-start.1 = (s32[240]{0:T(256)S(1)}, s32[240]{0:T(256)}, u32[]{:S(2)}) copy-start(s32[240]{0:T(256)} %param.6) | copy-start | bytes 2884
  0.0 1.3 %copy-start.2 = (s32[256]{0:T(256)S(1)}, s32[256]{0:T(256)}, u32[]{:S(2)}) copy-start(s32[256]{0:T(256)} %param.7) | copy-start | bytes 3076

commit v3 on v2

--- a/solution.py
+++ b/solution.py
@@ -12,7 +12,7 @@
 NO = 4
 NR = 2
 CHUNKS = 4
-ORDER = ((3, 2, 1, 0), (3, 0, 2, 1), (0, 3, 1, 2), (0, 1, 2, 3))
+ORDER = ((2, 3, 1, 0), (2, 3, 0, 1), (1, 0, 3, 2), (1, 0, 2, 3))
 PEERS = [(2, 0), (0, 1), (2, 1)]
 
 
@@ -28,11 +28,11 @@
         for v in ORDER[zz][:-1]:
             steps += [(v, c) for c in parts_of(zz, v)]
     else:
-        a, b, near, _ = ORDER[zz]
+        a, b, back, _ = ORDER[zz]
         timed = []
         for k in range(CHUNKS):
-            timed += [(k, 0, a, parts_of(zz, a)[k]), (k + 1.5, 1, b, parts_of(zz, b)[k]),
-                      (k + CHUNKS + 0.7, 2, near, parts_of(zz, near)[k])]
+            timed += [(k, 0, a, parts_of(zz, a)[k]), (k + CHUNKS + 0.7, 1, b, parts_of(zz, b)[k]),
+                      (k + CHUNKS + 2, 2, back, parts_of(zz, back)[k])]
         steps = [(v, c) for _, _, v, c in sorted(timed)]
     return steps + [(zz, c) for c in parts_of(zz, zz)]
 

time: 37 us -> 42.9 us (1.16)
  the two profiles are of different devices: /device:TPU:8 before, /device:TPU:0 now
where the time goes in v3:
time: 42.9 us; the launch traced here: 42.6 us
  Pallas kernels  40.5 us (94%)
  local copies, waits for them, and re-layouts  2.08 us (5%)
    pallas_call x1, Pallas kernels, on_lines(): pl.pallas_call(kernel, out_shape=jax.ShapeDtypeStruct((rows, width), jnp....  40.5 us
    unnamed x8, local copies, waits for them, and re-layouts  2.08 us

profile of v3, /device:TPU:0, one launch (start us, length us, event | category | flops | bytes accessed | tf_op | source)
XLA Modules:
  0.0 42.6 jit_solution(15012829866276853654)
XLA Ops:
  0.0 0.0 copy-start
  0.0 0.0 copy-start.1
  0.0 0.0 copy-start.2
  0.0 1.3 %copy.5.t_ref = bf16[512,480]{1,0:T(8,128)(2,1)S(1)} copy(bf16[512,480]{0,1:T(8,128)(2,1)} %param.4) | data formatting | bytes 983040 | tf_op args[0]
  1.3 0.0 copy-done
  1.3 0.0 copy-done.1
  1.3 0.0 copy-done.2
  1.3 40.5 %shard_map.46 = f32[512,256]{1,0:T(8,128)S(1)} custom-call(bf16[512,480]{1,0:T(8,128)(2,1)S(1)} %copy.5.t_ref, bf16[240,256]{1,0:T(8,128)(2,1)S(1)} %copy-done, s32[1,240]{1,0:T(1,128)S(1)} %bitcast.2, s32[1,256]{1,0:T(1,128)S(1)} %bitcast.3), custom_call_target="tpu_custom_call" | custom-call | flops 503316480 | bytes 737280 | tf_op jit(solution)/shard_map/pallas_call | solution.py:233
  41.8 0.8 %copy.7 = f32[512,256]{1,0:T(8,128)} copy(f32[512,256]{1,0:T(8,128)S(1)} %shard_map.46) | data formatting | bytes 1048576
Async XLA Ops:
  0.0 1.3 %copy-start = (bf16[240,256]{1,0:T(8,128)(2,1)S(1)}, bf16[240,256]{1,0:T(8,128)(2,1)}, u32[]{:S(2)}) copy-start(bf16[240,256]{1,0:T(8,128)(2,1)} %i_ref.1) | copy-start | bytes 368644
  0.0 1.3 %copy-start.1 = (s32[240]{0:T(256)S(1)}, s32[240]{0:T(256)}, u32[]{:S(2)}) copy-start(s32[240]{0:T(256)} %param.6) | copy-start | bytes 2884
  0.0 1.3 %copy-start.2 = (s32[256]{0:T(256)S(1)}, s32[256]{0:T(256)}, u32[]{:S(2)}) copy-start(s32[256]{0:T(256)} %param.7) | copy-start | bytes 3076
